TPU v7x, 512 devices: a whole 4x8x8 slice. The times are simulated.
512 devices in a mesh: row: 32 (over y, z_hi), col: 4 (over x), pair: 4 (over z_lo, core).
Axes of the slice: x: 4, y: 8, z: 8 (z_hi: 4, z_lo: 2; z = z_hi * 2 + z_lo), core: 2. Of those that a mesh axis runs over, the one named last changes fastest.
Arguments:
- amps: bfloat16 [512, 512, 512], P('pair', 'row', 'col'), may hold values from -6 to 6
- integrals: bfloat16 [4096, 512, 512], P('pair', 'row', 'col'), may hold values from -0.01171875 to 0.01171875
- mask_amps: int32 [8, 8], replicated, may hold values 0 or 1
- mask_ints: int32 [8, 8], replicated, may hold values 0 or 1
Outputs:
- residual: bfloat16 [512, 4096], P(('row', 'col'), 'pair')
All inputs are finite; a program needn't handle non-finite values.
Results may differ from a plain program's by a relative error of at most 0.00115.
Values may be sent and summed in bfloat16 or wider, within the bound.
A program may use at most 64 MiB of HBM per device.

v0:
```python
import jax
import jax.numpy as jnp
from jax import lax
from jax.sharding import PartitionSpec as P

TILE = 64
WIN = 64


def per_device(amps, integrals, mask_amps, mask_ints):
    local_pairs, local_c, local_d = amps.shape
    local_ab = integrals.shape[0]
    tiles = mask_amps.shape[0]
    c_global = lax.axis_index("row") * local_c + jnp.arange(local_c)
    d_global = lax.axis_index("col") * local_d + jnp.arange(local_d)
    onehot_c = (c_global[:, None] // TILE == jnp.arange(tiles)[None, :]).astype(jnp.float32)
    onehot_d = (d_global[:, None] // TILE == jnp.arange(tiles)[None, :]).astype(jnp.float32)
    both_masks = (mask_amps * mask_ints).astype(jnp.float32)
    factor = jnp.dot(jnp.dot(onehot_c, both_masks), onehot_d.T)
    masked = (amps * factor.astype(jnp.bfloat16)[None]).reshape(local_pairs, local_c * local_d)
    gathered = lax.all_gather(masked, "pair", axis=0, tiled=True)
    flat_ints = integrals.reshape(local_ab, local_c * local_d)
    ladder = lax.psum_scatter(
        lax.dot_general(
            gathered, flat_ints, (((1,), (1,)), ((), ())), preferred_element_type=jnp.float32
        ),
        ("row", "col"),
        scatter_dimension=0,
        tiled=True,
    )
    out_pairs = ladder.shape[0]
    groups = lax.axis_size("pair")
    width = WIN
    local_a = width // groups
    grid = ladder.reshape(out_pairs, local_a, groups, local_a)
    received = lax.all_to_all(grid, "pair", split_axis=2, concat_axis=2, tiled=True)
    swapped = jnp.transpose(received, (0, 3, 2, 1)).reshape(out_pairs, local_a * width)
    return (0.5 * (ladder - swapped)).astype(jnp.bfloat16)


def solution(mesh):
    return jax.shard_map(
        per_device,
        mesh=mesh,
        in_specs=(P("pair", "row", "col"), P("pair", "row", "col"), P(), P()),
        out_specs=P(("row", "col"), "pair"),
        check_vma=False,
    )
```

profile of v0, /device:TPU:1, one launch (start us, length us, event | category | flops | bytes accessed | tf_op | source)
XLA Modules:
  0.0 1531.3 jit_solution(5617520370174567015)
XLA Ops:
  6.5 0.0 all-gather.2.cloned.1.call-start
  6.6 1.0 fusion.6
  7.6 1.1 broadcast_multiply_fusion
  8.7 0.9 copy.15
  9.6 0.0 all-gather.2.cloned.1.call-update
  9.6 0.0 all-reduce.3.cloned.1.call-start
  9.7 40.6 %all-gather.2.cloned.1.call-done = bf16[512,2048]{1,0:T(8,128)(2,1)} async-done(((bf16[128,2048]{1,0:T(8,128)(2,1)}), bf16[512,2048]{1,0:T(8,128)(2,1)}) %all-gather.2.cloned.1.call-update) | async-done | bytes 2097168 | tf_op jit(solution)/shard_map/all_gather | solution.py:21
  50.3 6.5 fusion
  56.8 0.0 all-reduce.3.cloned.1.call-update
  56.8 1.3 dynamic-slice
  58.8 1370.6 %all-reduce.3.cloned.1.call-done = f32[512,1024]{1,0:T(8,128)} async-done(((f32[512,1024]{1,0:T(8,128)}), f32[512,1024]{1,0:T(8,128)}) %all-reduce.3.cloned.1.call-update) | async-done | bytes 2097168
  1429.4 0.8 constant_dynamic-slice_fusion
  1430.2 0.1 reshape.89
  1430.3 0.1 copy.6
  1430.4 0.1 reshape.92
  1430.5 91.0 %all_to_all.5 = f32[4,1,1024]{2,1,0:T(1,128)S(1)} all-to-all(f32[4,1,1024]{2,1,0:T(1,128)S(1)} %reshape.92), channel_id=1, replica_groups=mesh['row'=32,'col'=4,'pair'=4] {'pair'}, dimensions={0} | all-to-all | bytes 32768 | tf_op jit(solution)/shard_map/all_to_all | solution.py:36
  1521.6 0.5 broadcast.95
  1522.1 0.7 reduce
  1522.8 0.1 reshape.93
  1522.9 0.1 copy.7
  1523.0 0.1 reshape.90
  1523.1 1.4 multiply_convert_fusion
  (3 shorter events, 0.0 us)
Async XLA Ops:
  6.5 43.8 %all-gather.2.cloned.1.call-start = ((), (), s32[]{:S(2)}) async-start(), calls=%async_computation.1 | async-start | bytes 2621440 | tf_op jit(solution)/shard_map/all_gather | solution.py:21
  9.6 1419.8 %all-reduce.3.cloned.1.call-start = ((), (), s32[]{:S(2)}) async-start(), calls=%async_computation.2 | async-start | bytes 4194304
Sparse Core Ops, SparseCore 0:
  9.7 40.5 all-gather.1
  57.0 1372.3 all-reduce.2
where the time goes:
time: 1530 us
  waiting for transfers between devices  1410 us (92%)
  blocking collectives  91 us (6%)
    unnamed x3, waiting for transfers between devices  1370 us
    all_to_all x1, blocking collectives, per_device(): lax.all_to_all(grid, 'pair', split_axis=2, concat_axis=2, tiled=True)  91 us
    all_gather x1, waiting for transfers between devices, per_device(): gathered = lax.all_gather(masked, 'pair', axis=0, tiled=True)  40.6 us
  transfers between devices with their start and end apart: 2, of which 2 were waited for; matrix products, arithmetic and copies ran while one was open for 0% of the time, Pallas kernels for 0%

commit v1 on v0

v1 whole, which is shorter than its diff:
```python
import functools

import jax
import jax.numpy as jnp
from jax import lax
from jax.experimental import pallas as pl
from jax.experimental.pallas import tpu as pltpu
from jax.sharding import PartitionSpec as P

MESH = pl.DeviceIdType.MESH
NT_DIMS = (((1,), (1,)), ((), ()))
COLS = 768
PACKED = 512


def pack(v):
    top = jnp.maximum(jnp.max(jnp.abs(v), axis=1, keepdims=True), 1e-30)
    power = jnp.floor(jnp.log2(top)) + 1.0
    q = jnp.round(v * (jnp.exp2(15.0 - power) * 0.9999))
    q1, q2, q3 = q[:, 0:256], q[:, 256:512], q[:, 512:768]
    lane = lax.broadcasted_iota(jnp.int32, q3.shape, 1)
    q3 = jnp.where(lane == 120, power, q3)
    high = jnp.round(q3 * (1.0 / 256.0))
    low = q3 - 256.0 * high
    return jnp.concatenate([q1 * 512.0 + high, q2 * 512.0 + low], axis=1)


def unpack(w):
    w1, w2 = w[:, 0:256], w[:, 256:512]
    q1 = jnp.round(w1 * (1.0 / 512.0))
    q2 = jnp.round(w2 * (1.0 / 512.0))
    q3 = 256.0 * (w1 - 512.0 * q1) + (w2 - 512.0 * q2)
    power = q3[:, 120:121]
    scale = jnp.exp2(power - 15.0) * (1.0 / 0.9999)
    return jnp.concatenate([q1, q2, q3], axis=1) * scale


def store_group(slabs, dst, row):
    turned = jnp.swapaxes(slabs, 0, 1)
    for c in range(16):
        dst[pl.ds(row, 16), c * 128 : (c + 1) * 128] = turned[c]


def kernel(
    amps, ints, mask_a, mask_i, out,
    raw, ints_v, rcore, flat_a, flat_i, part, xsend, xrecv, ysend, yrecv, yown,
    zs, zsame, znbr, zq, place,
    lsem, asend, arecv, isend, irecv, xss, xrs, yss, yrs, zss, zrs,
):
    row, x, pair = lax.axis_index("row"), lax.axis_index("col"), lax.axis_index("pair")
    y, zh = row // 4, row % 4
    zl, c = pair // 2, pair % 2
    pn = 2 * zl + 1 - c

    def dev(y_=None, zh_=None, x_=None, pair_=None):
        yy = y if y_ is None else y_
        zz = zh if zh_ is None else zh_
        return {
            "row": yy * 4 + zz,
            "col": x if x_ is None else x_,
            "pair": pair if pair_ is None else pair_,
        }

    core_dev = dev(pair_=pn)
    zl_dev = dev(pair_=2 * (1 - zl) + c)

    def remote(src, dst, ss, rs, device):
        return pltpu.make_async_remote_copy(src, dst, ss, rs, device_id=device, device_id_type=MESH)

    barrier = pltpu.get_barrier_semaphore()
    peers = [dev(x_=(x + j) % 4) for j in range(1, 4)]
    peers += [dev(y_=(y + j) % 8) for j in range(1, 8)]
    peers += [
        dev(zh_=(zh + jz) % 4, pair_=(pair + jp) % 4) for jz in range(4) for jp in range(4) if jz or jp
    ]
    for device in peers:
        pl.semaphore_signal(barrier, inc=1, device_id=device, device_id_type=MESH)

    own_copy = pltpu.make_async_copy(amps, raw.at[0], lsem.at[0])
    own_copy.start()
    ints_copy = pltpu.make_async_copy(ints, ints_v, lsem.at[1])
    ints_copy.start()
    pl.semaphore_wait(barrier, len(peers))

    sends = []
    core_amps = remote(amps, raw.at[1], asend.at[0], arecv.at[0], core_dev)
    core_amps.start()
    sends.append(core_amps)
    zcopies = []
    for k in range(4):
        cp = remote(amps.at[pl.ds(32 * k, 32)], raw.at[2, pl.ds(32 * k, 32)], asend.at[1 + k], arecv.at[1 + k], zl_dev)
        cp.start()
        zcopies.append(cp)
        sends.append(cp)
    icopies = []
    for a in range(2):
        vh = (a + 1 + c) % 2
        cp = remote(
            ints.at[pl.ds(8 * a, 8), pl.ds(16 * pn + 8 * vh, 8)], rcore.at[a], isend.at[a], irecv.at[a], core_dev
        )
        cp.start()
        icopies.append(cp)
        sends.append(cp)

    m0 = (mask_a[y, 2 * x] * mask_i[y, 2 * x]).astype(jnp.float32)
    m1 = (mask_a[y, 2 * x + 1] * mask_i[y, 2 * x + 1]).astype(jnp.float32)
    lane = lax.broadcasted_iota(jnp.int32, (16, 128), 1)
    factor = jnp.where(lane < 64, m0, m1).astype(jnp.bfloat16)

    def amps_rows(first, second, k, xq, dst_row):
        parts = [
            raw[src, pl.ds(32 * k + 16 * zb + 4 * xq, 4)] for src in (first, second) for zb in range(2)
        ]
        store_group(jnp.concatenate(parts, axis=0) * factor[None], flat_a, dst_row)

    def ints_rows(slabs, dst_row):
        store_group(jnp.concatenate([ints_v[a, pl.ds(b, 1)] for a, b in slabs], axis=0), flat_i, dst_row)

    own_copy.wait()
    ints_copy.wait()

    def cross(g, _):
        for j in range(2):
            q = 2 * (1 - zl) + j
            slabs = [((1 - zl) * g + zl * r, 16 * q + (1 - zl) * r + zl * g) for r in range(16)]
            ints_rows(slabs, pl.multiple_of(256 * j + 16 * g, 16))
        return 0

    lax.fori_loop(0, 16, cross, 0)

    def diagonal(g, _):
        turn = [(r + g + 1) % 16 for r in range(16)]
        ints_rows([(r, 16 * pair + turn[r]) for r in range(16)], pl.multiple_of(512 + 16 * g, 16))
        ints_rows([(turn[r], 16 * pair + r) for r in range(16)], pl.multiple_of(768 + 16 * g, 16))
        half = g // 4
        vh = (half + c) % 2
        slabs = [(8 * half + 2 * (g % 4) + r // 8, 16 * pn + 8 * vh + r % 8) for r in range(16)]
        ints_rows(slabs, pl.multiple_of(640 + 16 * g, 16))
        return 0

    lax.fori_loop(0, 8, diagonal, 0)
    for cp in icopies:
        cp.wait_recv()

    def minus(g, _):
        half = (g // 4 + c) % 2
        slabs = [rcore[half, r % 8, pl.ds(2 * (g % 4) + r // 8, 1)] for r in range(16)]
        store_group(jnp.concatenate(slabs, axis=0), flat_i, pl.multiple_of(896 + 16 * g, 16))
        return 0

    lax.fori_loop(0, 8, minus, 0)
    core_amps.wait_recv()

    def early_rows(n, _):
        amps_rows(0, 1, n // 4, n % 4, pl.multiple_of(16 * n, 16))
        return 0

    lax.fori_loop(0, 16, early_rows, 0)

    def ladder(row0, rows):
        a = flat_a[row0 : row0 + rows, :]
        for n in range(2):
            part[row0 : row0 + rows, 256 * n : 256 * (n + 1)] = lax.dot_general(
                a, flat_i[256 * n : 256 * (n + 1), :], NT_DIMS, preferred_element_type=jnp.float32
            )
        plus = lax.dot_general(a, flat_i[512:768, :], NT_DIMS, preferred_element_type=jnp.float32)
        less = lax.dot_general(a, flat_i[768:1024, :], NT_DIMS, preferred_element_type=jnp.float32)
        part[row0 : row0 + rows, 512:768] = plus - less

    def xcopy(s, j):
        to = (x + j) % 4
        return remote(
            xsend.at[s, to], xrecv.at[s, j - 1], xss.at[s, j - 1], xrs.at[s, j - 1], dev(x_=to)
        )

    def send_x(s):
        packed = pack(part[64 * s : 64 * s + 64, :])
        for xq in range(4):
            xsend[s, xq] = packed[16 * xq : 16 * xq + 16]
        for j in (2, 1, 3):
            xcopy(s, j).start()

    def ydest(s, slot):
        k = s % 4
        zsrc = zl if s < 4 else 1 - zl
        p = 2 * zsrc + (c if slot == 0 else 1 - c)
        to = 2 * p + k // 2
        return to, (y - to + 8) % 8, k % 2

    def ycopy(s, slot):
        to, j, h = ydest(s, slot)
        return remote(ysend.at[s, slot], yrecv.at[h, j], yss.at[s, slot], yrs.at[h, j], dev(y_=to))

    def reduce_x(s):
        for j in (1, 3, 2):
            xcopy(s, j).wait_recv()
        total = part[pl.ds(pl.multiple_of(64 * s + 16 * x, 16), 16), :]
        for j in (1, 3, 2):
            total = total + unpack(xrecv[s, j - 1])
        packed = pack(total)
        for slot in range(2):
            ysend[s, slot] = packed[8 * slot : 8 * slot + 8]
            _, j, h = ydest(s, slot)

            @pl.when(j != 0)
            def _():
                ycopy(s, slot).start()

            @pl.when(j == 0)
            def _():
                yown[h] = total[8 * slot : 8 * slot + 8]

    ladder(0, 256)
    for s in range(4):
        send_x(s)

    def build_place():
        col = lax.broadcasted_iota(jnp.int32, (1, 1024), 1)
        u, b = col // 64, col % 64
        block, v = b // 16, b % 16
        turn = (v - u + 16) % 16
        diag_plus = jnp.logical_or(turn < 8, jnp.logical_and(turn == 8, u < 8))
        src = jnp.where(diag_plus, 512 + (turn - 1) * 16 + u, 512 + (15 - turn) * 16 + v)
        sign = jnp.where(diag_plus, 1.0, -1.0)
        src = jnp.where(turn == 0, -1, src)
        uh, vh, u8, v8 = u // 8, v // 8, u % 8, v % 8
        mine = (uh + vh) % 2 == c
        near = block == pn
        src = jnp.where(near, jnp.where(mine, 640 + uh * 64 + u8 * 8 + v8, 768 + vh * 64 + v8 * 8 + u8), src)
        sign = jnp.where(near, jnp.where(mine, 1.0, -1.0), sign)
        far = block // 2 == 1 - zl
        src = jnp.where(far, (block % 2) * 256 + (1 - zl) * (u * 16 + v) + zl * (v * 16 + u), src)
        sign = jnp.where(far, 1.0, sign)

        def body(r, _):
            rows = r * 64 + lax.broadcasted_iota(jnp.int32, (64, 1024), 0)
            picked = jnp.where(rows == src, sign, 0.0)
            place[pl.ds(pl.multiple_of(r * 64, 64), 64), :] = picked.astype(jnp.bfloat16)
            return 0

        lax.fori_loop(0, 14, body, 0)

    build_place()

    fwds = []
    for k in range(4):
        s = 4 + k
        zcopies[k].wait_recv()
        fwd = remote(
            raw.at[2, pl.ds(32 * k, 32)], raw.at[3, pl.ds(32 * k, 32)], asend.at[5 + k], arecv.at[5 + k], core_dev
        )
        fwd.start()
        fwds.append(fwd)
        if k == 1:
            reduce_x(0)
        if k == 2:
            reduce_x(1)
        if k == 3:
            reduce_x(2)
            reduce_x(3)
        fwd.wait_recv()

        def late_rows(n, _):
            amps_rows(2, 3, k, n, pl.multiple_of(64 * s + 16 * n, 16))
            return 0

        lax.fori_loop(0, 4, late_rows, 0)
        ladder(64 * s, 64)
        send_x(s)
    for s in range(4, 8):
        reduce_x(s)

    for h in range(2):
        total = yown[h]
        for j in range(1, 8):
            remote(ysend.at[0, 0], yrecv.at[h, j], yss.at[0, 0], yrs.at[h, j], core_dev).wait_recv()
            total = total + unpack(yrecv[h, j])
        for zb in range(2):
            zs[2 * h + zb] = total[4 * zb : 4 * zb + 4]

    zcps = []
    for jz in (2, 1, 3, 0):
        to = (zh + jz) % 4
        for j in range(2):
            zcps.append(
                remote(
                    zs.at[to, :, pl.ds(256 * j, 256)], zq.at[c, jz], zss.at[jz, j], zrs.at[jz, c],
                    dev(zh_=to, pair_=2 * (1 - zl) + j),
                )
            )
        if jz:
            zcps.append(remote(zs.at[to], zsame.at[jz - 1], zss.at[jz, 2], zrs.at[jz, 2], dev(zh_=to)))
        zcps.append(
            remote(zs.at[to, :, pl.ds(640, 128)], znbr.at[jz], zss.at[jz, 3], zrs.at[jz, 3], dev(zh_=to, pair_=pn))
        )
    for cp in zcps:
        cp.start()

    for cp in sends + fwds:
        cp.wait_send()
    for s in range(8):
        for j in range(1, 4):
            xcopy(s, j).wait_send()
        for slot in range(2):
            @pl.when(ydest(s, slot)[1] != 0)
            def _():
                ycopy(s, slot).wait_send()

    same = zs[zh]
    for jz in range(1, 4):
        remote(zs.at[0], zsame.at[jz - 1], zss.at[jz, 2], zrs.at[jz, 2], core_dev).wait_recv()
        same = same + zsame[jz - 1]
    near = None
    for jz in range(4):
        remote(zs.at[0, :, pl.ds(0, 128)], znbr.at[jz], zss.at[jz, 3], zrs.at[jz, 3], core_dev).wait_recv()
        near = znbr[jz] if near is None else near + znbr[jz]
    far = []
    for j in range(2):
        got = None
        for jz in range(4):
            remote(zs.at[0, :, pl.ds(0, 256)], zq.at[j, jz], zss.at[jz, j], zrs.at[jz, j], core_dev).wait_recv()
            got = zq[j, jz] if got is None else got + zq[j, jz]
        far.append(got)
    values = jnp.concatenate(
        [same[:, 0:256] - far[0], same[:, 256:512] - far[1], same[:, 512:768], near], axis=1
    )
    values = (0.5 * values).astype(jnp.bfloat16)
    out[...] = jnp.dot(values, place[...], preferred_element_type=jnp.float32).astype(jnp.bfloat16)
    for cp in zcps:
        cp.wait_send()


def per_device(amps, integrals, mask_amps, mask_ints):
    ints = integrals.reshape(16, 64, 16, 128)
    bf, f32 = jnp.bfloat16, jnp.float32
    dma = pltpu.SemaphoreType.DMA
    return pl.pallas_call(
        kernel,
        out_shape=jax.ShapeDtypeStruct((4, 1024), bf),
        in_specs=[pl.BlockSpec(memory_space=pl.ANY)] * 2 + [pl.BlockSpec(memory_space=pltpu.SMEM)] * 2,
        out_specs=pl.BlockSpec(memory_space=pltpu.VMEM),
        scratch_shapes=[
            pltpu.VMEM((4, 128, 16, 128), bf),
            pltpu.VMEM((16, 64, 16, 128), bf),
            pltpu.VMEM((2, 8, 8, 16, 128), bf),
            pltpu.VMEM((512, 2048), bf),
            pltpu.VMEM((1024, 2048), bf),
            pltpu.VMEM((512, COLS), f32),
            pltpu.VMEM((8, 4, 16, PACKED), f32),
            pltpu.VMEM((8, 3, 16, PACKED), f32),
            pltpu.VMEM((8, 2, 8, PACKED), f32),
            pltpu.VMEM((2, 8, 8, PACKED), f32),
            pltpu.VMEM((2, 8, COLS), f32),
            pltpu.VMEM((4, 4, COLS), f32),
            pltpu.VMEM((3, 4, COLS), f32),
            pltpu.VMEM((4, 4, 128), f32),
            pltpu.VMEM((2, 4, 4, 256), f32),
            pltpu.VMEM((896, 1024), bf),
            dma((2,)), dma((9,)), dma((9,)), dma((2,)), dma((2,)),
            dma((8, 3)), dma((8, 3)), dma((8, 2)), dma((2, 8)), dma((4, 4)), dma((4, 4)),
        ],
        compiler_params=pltpu.CompilerParams(
            collective_id=0, has_side_effects=True, vmem_limit_bytes=48 * 2**20
        ),
        cost_estimate=pl.CostEstimate(flops=2 * 512 * 1024 * 2048, bytes_accessed=5 * 2**20, transcendentals=0),
    )(amps, ints, mask_amps, mask_ints)


def solution(mesh):
    return jax.shard_map(
        per_device,
        mesh=mesh,
        in_specs=(P("pair", "row", "col"), P("pair", "row", "col"), P(), P()),
        out_specs=P(("row", "col"), "pair"),
        check_vma=False,
    )
```

time: 1530 us -> 52.4 us (0.03)
  the two profiles are of different devices: /device:TPU:1 before, /device:TPU:9 now
where the time goes in v1:
time: 52.4 us; the launch traced here: 52.2 us
  Pallas kernels  47 us (90%)
  local copies, waits for them, and re-layouts  5.2 us (10%)
    pallas_call x1, Pallas kernels, per_device(): pl.pallas_call(kernel, out_shape=jax.ShapeDtypeStruct((4, 1024), bf), in_...  47 us
    unnamed x9, local copies, waits for them, and re-layouts  5.2 us

profile of v1, /device:TPU:9, one launch (start us, length us, event | category | flops | bytes accessed | tf_op | source)
XLA Modules:
  0.0 52.2 jit_solution(10569693948178048581)
XLA Ops:
  0.0 0.0 copy-start
  0.0 2.2 %copy-done = bf16[1024,16,128]{2,1,0:T(8,128)(2,1)S(1)} copy-done((bf16[1024,16,128]{2,1,0:T(8,128)(2,1)S(1)}, bf16[1024,16,128]{2,1,0:T(8,128)(2,1)}, u32[]{:S(2)}) %copy-start) | copy-done | bytes 4194328
  2.2 0.0 copy-start.1
  2.2 1.0 %copy-done.1 = bf16[128,16,128]{2,1,0:T(8,128)(2,1)S(1)} copy-done((bf16[128,16,128]{2,1,0:T(8,128)(2,1)S(1)}, bf16[128,16,128]{2,1,0:T(8,128)(2,1)}, u32[]{:S(2)}) %copy-start.1) | copy-done | bytes 524312
  3.2 0.0 copy-start.2
  3.2 0.7 %copy-done.2 = s32[8,8]{1,0:T(8,128)S(1)} copy-done((s32[8,8]{1,0:T(8,128)S(1)}, s32[8,8]{1,0:T(8,128)}, u32[]{:S(2)}) %copy-start.2) | copy-done | bytes 280
  3.9 0.0 copy-start.3
  3.9 0.7 %copy-done.3 = s32[8,8]{1,0:T(8,128)S(1)} copy-done((s32[8,8]{1,0:T(8,128)S(1)}, s32[8,8]{1,0:T(8,128)}, u32[]{:S(2)}) %copy-start.3) | copy-done | bytes 280
  4.6 47.0 %shard_map.46 = bf16[4,1024]{1,0:T(4,128)(2,1)S(1)} custom-call(bf16[128,16,128]{2,1,0:T(8,128)(2,1)S(1)} %copy-done.1, bf16[16,64,16,128]{3,2,1,0:T(8,128)(2,1)S(1)} %bitcast.1, s32[8,8]{1,0:T(8,128)S(1)} %copy-done.2, s32[8,8]{1,0:T(8,128)S(1)} %copy-done.3), custom_call_target="tpu_custom_call" | custom-call | flops 2147483648 | bytes 5242880 | tf_op jit(solution)/shard_map/pallas_call | solution.py:337
  51.6 0.6 %copy.6 = bf16[4,1024]{1,0:T(4,128)(2,1)} copy(bf16[4,1024]{1,0:T(4,128)(2,1)S(1)} %shard_map.46) | data formatting | bytes 16384
Async XLA Ops:
  0.0 2.2 %copy-start = (bf16[1024,16,128]{2,1,0:T(8,128)(2,1)S(1)}, bf16[1024,16,128]{2,1,0:T(8,128)(2,1)}, u32[]{:S(2)}) copy-start(bf16[1024,16,128]{2,1,0:T(8,128)(2,1)} %param.5) | copy-start | bytes 12582916
  2.2 1.0 %copy-start.1 = (bf16[128,16,128]{2,1,0:T(8,128)(2,1)S(1)}, bf16[128,16,128]{2,1,0:T(8,128)(2,1)}, u32[]{:S(2)}) copy-start(bf16[128,16,128]{2,1,0:T(8,128)(2,1)} %amps.1) | copy-start | bytes 1572868
  3.2 0.7 %copy-start.2 = (s32[8,8]{1,0:T(8,128)S(1)}, s32[8,8]{1,0:T(8,128)}, u32[]{:S(2)}) copy-start(s32[8,8]{1,0:T(8,128)} %mask_a.1) | copy-start | bytes 772
  3.9 0.7 %copy-start.3 = (s32[8,8]{1,0:T(8,128)S(1)}, s32[8,8]{1,0:T(8,128)}, u32[]{:S(2)}) copy-start(s32[8,8]{1,0:T(8,128)} %mask_i.1) | copy-start | bytes 772

commit v2 on v1

--- a/solution.py
+++ b/solution.py
@@ -42,8 +42,8 @@
 
 
 def kernel(
-    amps, ints, mask_a, mask_i, out,
-    raw, ints_v, rcore, flat_a, flat_i, part, xsend, xrecv, ysend, yrecv, yown,
+    amps, ints, mask_a_hbm, mask_i_hbm, out,
+    mask_a, mask_i, raw, ints_v, rcore, flat_a, flat_i, part, xsend, xrecv, ysend, yrecv, yown,
     zs, zsame, znbr, zq, place,
     lsem, asend, arecv, isend, irecv, xss, xrs, yss, yrs, zss, zrs,
 ):
@@ -64,6 +64,9 @@
     core_dev = dev(pair_=pn)
     zl_dev = dev(pair_=2 * (1 - zl) + c)
 
+    def first_row(k, zb):
+        return 64 * (k // 2) + 32 * zb + 16 * (k % 2)
+
     def remote(src, dst, ss, rs, device):
         return pltpu.make_async_remote_copy(src, dst, ss, rs, device_id=device, device_id_type=MESH)
 
@@ -80,6 +83,12 @@
     own_copy.start()
     ints_copy = pltpu.make_async_copy(ints, ints_v, lsem.at[1])
     ints_copy.start()
+    mask_copies = [
+        pltpu.make_async_copy(mask_a_hbm, mask_a, lsem.at[2]),
+        pltpu.make_async_copy(mask_i_hbm, mask_i, lsem.at[3]),
+    ]
+    for cp in mask_copies:
+        cp.start()
     pl.semaphore_wait(barrier, len(peers))
 
     sends = []
@@ -87,8 +96,9 @@
     core_amps.start()
     sends.append(core_amps)
     zcopies = []
-    for k in range(4):
-        cp = remote(amps.at[pl.ds(32 * k, 32)], raw.at[2, pl.ds(32 * k, 32)], asend.at[1 + k], arecv.at[1 + k], zl_dev)
+    for n in range(8):
+        at = pl.ds(first_row(n // 2, n % 2), 16)
+        cp = remote(amps.at[at], raw.at[2, at], asend.at[1 + n], arecv.at[1 + n], zl_dev)
         cp.start()
         zcopies.append(cp)
         sends.append(cp)
@@ -102,6 +112,8 @@
         icopies.append(cp)
         sends.append(cp)
 
+    for cp in mask_copies:
+        cp.wait()
     m0 = (mask_a[y, 2 * x] * mask_i[y, 2 * x]).astype(jnp.float32)
     m1 = (mask_a[y, 2 * x + 1] * mask_i[y, 2 * x + 1]).astype(jnp.float32)
     lane = lax.broadcasted_iota(jnp.int32, (16, 128), 1)
@@ -109,7 +121,7 @@
 
     def amps_rows(first, second, k, xq, dst_row):
         parts = [
-            raw[src, pl.ds(32 * k + 16 * zb + 4 * xq, 4)] for src in (first, second) for zb in range(2)
+            raw[src, pl.ds(first_row(k, zb) + 4 * xq, 4)] for src in (first, second) for zb in range(2)
         ]
         store_group(jnp.concatenate(parts, axis=0) * factor[None], flat_a, dst_row)
 
@@ -245,12 +257,12 @@
     fwds = []
     for k in range(4):
         s = 4 + k
-        zcopies[k].wait_recv()
-        fwd = remote(
-            raw.at[2, pl.ds(32 * k, 32)], raw.at[3, pl.ds(32 * k, 32)], asend.at[5 + k], arecv.at[5 + k], core_dev
-        )
-        fwd.start()
-        fwds.append(fwd)
+        for n in (2 * k, 2 * k + 1):
+            zcopies[n].wait_recv()
+            at = pl.ds(first_row(k, n % 2), 16)
+            fwd = remote(raw.at[2, at], raw.at[3, at], asend.at[9 + n], arecv.at[9 + n], core_dev)
+            fwd.start()
+            fwds.append(fwd)
         if k == 1:
             reduce_x(0)
         if k == 2:
@@ -258,7 +270,8 @@
         if k == 3:
             reduce_x(2)
             reduce_x(3)
-        fwd.wait_recv()
+        for fwd in fwds[2 * k :]:
+            fwd.wait_recv()
 
         def late_rows(n, _):
             amps_rows(2, 3, k, n, pl.multiple_of(64 * s + 16 * n, 16))
@@ -269,6 +282,20 @@
         send_x(s)
     for s in range(4, 8):
         reduce_x(s)
+
+    def zcopies_of(to, n):
+        jz = (to - zh + 4) % 4
+        far = [
+            remote(
+                zs.at[to, :, pl.ds(256 * j, 256)], zq.at[c, jz], zss.at[n, j], zrs.at[jz, c],
+                dev(zh_=to, pair_=2 * (1 - zl) + j),
+            )
+            for j in range(2)
+        ]
+        near = remote(
+            zs.at[to, :, pl.ds(640, 128)], znbr.at[jz], zss.at[n, 3], zrs.at[jz, 3], dev(zh_=to, pair_=pn)
+        )
+        return jz, far + [near], remote(zs.at[to], zsame.at[jz], zss.at[n, 2], zrs.at[jz, 2], dev(zh_=to))
 
     for h in range(2):
         total = yown[h]
@@ -276,25 +303,16 @@
             remote(ysend.at[0, 0], yrecv.at[h, j], yss.at[0, 0], yrs.at[h, j], core_dev).wait_recv()
             total = total + unpack(yrecv[h, j])
         for zb in range(2):
-            zs[2 * h + zb] = total[4 * zb : 4 * zb + 4]
-
-    zcps = []
-    for jz in (2, 1, 3, 0):
-        to = (zh + jz) % 4
-        for j in range(2):
-            zcps.append(
-                remote(
-                    zs.at[to, :, pl.ds(256 * j, 256)], zq.at[c, jz], zss.at[jz, j], zrs.at[jz, c],
-                    dev(zh_=to, pair_=2 * (1 - zl) + j),
-                )
-            )
-        if jz:
-            zcps.append(remote(zs.at[to], zsame.at[jz - 1], zss.at[jz, 2], zrs.at[jz, 2], dev(zh_=to)))
-        zcps.append(
-            remote(zs.at[to, :, pl.ds(640, 128)], znbr.at[jz], zss.at[jz, 3], zrs.at[jz, 3], dev(zh_=to, pair_=pn))
-        )
-    for cp in zcps:
-        cp.start()
+            zs[2 * zb + h] = total[4 * zb : 4 * zb + 4]
+        for zb in range(2):
+            jz, copies, same_copy = zcopies_of(2 * zb + h, 2 * zb + h)
+
+            @pl.when(jz != 0)
+            def _():
+                same_copy.start()
+
+            for cp in copies:
+                cp.start()
 
     for cp in sends + fwds:
         cp.wait_send()
@@ -308,8 +326,8 @@
 
     same = zs[zh]
     for jz in range(1, 4):
-        remote(zs.at[0], zsame.at[jz - 1], zss.at[jz, 2], zrs.at[jz, 2], core_dev).wait_recv()
-        same = same + zsame[jz - 1]
+        remote(zs.at[0], zsame.at[jz], zss.at[jz, 2], zrs.at[jz, 2], core_dev).wait_recv()
+        same = same + zsame[jz]
     near = None
     for jz in range(4):
         remote(zs.at[0, :, pl.ds(0, 128)], znbr.at[jz], zss.at[jz, 3], zrs.at[jz, 3], core_dev).wait_recv()
@@ -326,8 +344,14 @@
     )
     values = (0.5 * values).astype(jnp.bfloat16)
     out[...] = jnp.dot(values, place[...], preferred_element_type=jnp.float32).astype(jnp.bfloat16)
-    for cp in zcps:
-        cp.wait_send()
+    for n in range(4):
+        jz, copies, same_copy = zcopies_of(n, n)
+        for cp in copies:
+            cp.wait_send()
+
+        @pl.when(jz != 0)
+        def _():
+            same_copy.wait_send()
 
 
 def per_device(amps, integrals, mask_amps, mask_ints):
@@ -337,9 +361,11 @@
     return pl.pallas_call(
         kernel,
         out_shape=jax.ShapeDtypeStruct((4, 1024), bf),
-        in_specs=[pl.BlockSpec(memory_space=pl.ANY)] * 2 + [pl.BlockSpec(memory_space=pltpu.SMEM)] * 2,
+        in_specs=[pl.BlockSpec(memory_space=pltpu.HBM)] * 4,
         out_specs=pl.BlockSpec(memory_space=pltpu.VMEM),
         scratch_shapes=[
+            pltpu.SMEM((8, 8), jnp.int32),
+            pltpu.SMEM((8, 8), jnp.int32),
             pltpu.VMEM((4, 128, 16, 128), bf),
             pltpu.VMEM((16, 64, 16, 128), bf),
             pltpu.VMEM((2, 8, 8, 16, 128), bf),
@@ -352,15 +378,15 @@
             pltpu.VMEM((2, 8, 8, PACKED), f32),
             pltpu.VMEM((2, 8, COLS), f32),
             pltpu.VMEM((4, 4, COLS), f32),
-            pltpu.VMEM((3, 4, COLS), f32),
+            pltpu.VMEM((4, 4, COLS), f32),
             pltpu.VMEM((4, 4, 128), f32),
             pltpu.VMEM((2, 4, 4, 256), f32),
             pltpu.VMEM((896, 1024), bf),
-            dma((2,)), dma((9,)), dma((9,)), dma((2,)), dma((2,)),
+            dma((4,)), dma((17,)), dma((17,)), dma((2,)), dma((2,)),
             dma((8, 3)), dma((8, 3)), dma((8, 2)), dma((2, 8)), dma((4, 4)), dma((4, 4)),
         ],
         compiler_params=pltpu.CompilerParams(
-            collective_id=0, has_side_effects=True, vmem_limit_bytes=48 * 2**20
+            collective_id=0, has_side_effects=True, vmem_limit_bytes=61 * 2**20
         ),
         cost_estimate=pl.CostEstimate(flops=2 * 512 * 1024 * 2048, bytes_accessed=5 * 2**20, transcendentals=0),
     )(amps, ints, mask_amps, mask_ints)

time: 52.4 us -> 46.8 us (0.89)
  local copies, waits for them, and re-layouts: 5.2 us -> 1.3 us
  Pallas kernels: 47 us -> 45.3 us
    unnamed x9 -> x1, local copies, waits for them, and re-layouts: 5.2 us -> 1.3 us
    pallas_call x1, Pallas kernels: 47 us -> 45.3 us  [per_device(): pl.pallas_call(kernel, out_shape=jax.ShapeDtypeStruct((4, 1024), bf), in_...]
where the time goes in v2:
time: 46.8 us; the launch traced here: 46.6 us
  Pallas kernels  45.3 us (97%)
  local copies, waits for them, and re-layouts  1.3 us (3%)
    pallas_call x1, Pallas kernels, per_device(): pl.pallas_call(kernel, out_shape=jax.ShapeDtypeStruct((4, 1024), bf), in_...  45.3 us
    unnamed x1, local copies, waits for them, and re-layouts  1.3 us

profile of v2, /device:TPU:9, one launch (start us, length us, event | category | flops | bytes accessed | tf_op | source)
XLA Modules:
  0.0 46.6 jit_solution(18101306250331735677)
XLA Ops:
  0.0 45.3 %shard_map.46 = bf16[4,1024]{1,0:T(4,128)(2,1)} custom-call(bf16[128,16,128]{2,1,0:T(8,128)(2,1)} %amps.1, bf16[16,64,16,128]{3,2,1,0:T(8,128)(2,1)} %bitcast.1, s32[8,8]{1,0:T(8,128)} %mask_a_hbm.1, s32[8,8]{1,0:T(8,128)} %mask_i_hbm.1), custom_call_target="tpu_custom_call" | custom-call | flops 2147483648 | bytes 5242880 | tf_op jit(solution)/shard_map/pallas_call | solution.py:361
  45.3 1.3 %copy.6 = bf16[4,1024]{1,0:T(4,128)(2,1)} copy(bf16[4,1024]{1,0:T(4,128)(2,1)} %shard_map.46) | data formatting | bytes 16384

commit v3 on v2

--- a/solution.py
+++ b/solution.py
@@ -43,7 +43,7 @@
 
 def kernel(
     amps, ints, mask_a_hbm, mask_i_hbm, out,
-    mask_a, mask_i, raw, ints_v, rcore, flat_a, flat_i, part, xsend, xrecv, ysend, yrecv, yown,
+    mask_a, mask_i, raw, ints_v, rcore, flat_a, flat_i, flat_t, part, xsend, xrecv, ysend, yrecv, yown,
     zs, zsame, znbr, zq, place,
     lsem, asend, arecv, isend, irecv, xss, xrs, yss, yrs, zss, zrs,
 ):
@@ -138,7 +138,7 @@
             ints_rows(slabs, pl.multiple_of(256 * j + 16 * g, 16))
         return 0
 
-    lax.fori_loop(0, 16, cross, 0)
+    lax.fori_loop(0, 16, cross, 0, unroll=2)
 
     def diagonal(g, _):
         turn = [(r + g + 1) % 16 for r in range(16)]
@@ -150,7 +150,7 @@
         ints_rows(slabs, pl.multiple_of(640 + 16 * g, 16))
         return 0
 
-    lax.fori_loop(0, 8, diagonal, 0)
+    lax.fori_loop(0, 8, diagonal, 0, unroll=2)
     for cp in icopies:
         cp.wait_recv()
 
@@ -160,24 +160,25 @@
         store_group(jnp.concatenate(slabs, axis=0), flat_i, pl.multiple_of(896 + 16 * g, 16))
         return 0
 
-    lax.fori_loop(0, 8, minus, 0)
+    lax.fori_loop(0, 8, minus, 0, unroll=4)
     core_amps.wait_recv()
 
     def early_rows(n, _):
         amps_rows(0, 1, n // 4, n % 4, pl.multiple_of(16 * n, 16))
         return 0
 
-    lax.fori_loop(0, 16, early_rows, 0)
-
-    def ladder(row0, rows):
+    lax.fori_loop(0, 16, early_rows, 0, unroll=4)
+
+    def ladder(row0, rows, turned=False):
         a = flat_a[row0 : row0 + rows, :]
+        def columns(first):
+            if turned:
+                return jnp.dot(a, flat_t[:, first : first + 256], preferred_element_type=jnp.float32)
+            return lax.dot_general(a, flat_i[first : first + 256, :], NT_DIMS, preferred_element_type=jnp.float32)
+
         for n in range(2):
-            part[row0 : row0 + rows, 256 * n : 256 * (n + 1)] = lax.dot_general(
-                a, flat_i[256 * n : 256 * (n + 1), :], NT_DIMS, preferred_element_type=jnp.float32
-            )
-        plus = lax.dot_general(a, flat_i[512:768, :], NT_DIMS, preferred_element_type=jnp.float32)
-        less = lax.dot_general(a, flat_i[768:1024, :], NT_DIMS, preferred_element_type=jnp.float32)
-        part[row0 : row0 + rows, 512:768] = plus - less
+            part[row0 : row0 + rows, 256 * n : 256 * (n + 1)] = columns(256 * n)
+        part[row0 : row0 + rows, 512:768] = columns(512) - columns(768)
 
     def xcopy(s, j):
         to = (x + j) % 4
@@ -252,7 +253,12 @@
 
         lax.fori_loop(0, 14, body, 0)
 
-    build_place()
+    def turn_ints(n, _):
+        rows, cols = pl.multiple_of(n % 4 * 256, 256), pl.multiple_of(n // 4 * 256, 256)
+        flat_t[pl.ds(cols, 256), pl.ds(rows, 256)] = flat_i[pl.ds(rows, 256), pl.ds(cols, 256)].T
+        return 0
+
+    lax.fori_loop(0, 32, turn_ints, 0, unroll=2)
 
     fwds = []
     for k in range(4):
@@ -277,11 +283,12 @@
             amps_rows(2, 3, k, n, pl.multiple_of(64 * s + 16 * n, 16))
             return 0
 
-        lax.fori_loop(0, 4, late_rows, 0)
-        ladder(64 * s, 64)
+        lax.fori_loop(0, 4, late_rows, 0, unroll=4)
+        ladder(64 * s, 64, True)
         send_x(s)
     for s in range(4, 8):
         reduce_x(s)
+    build_place()
 
     def zcopies_of(to, n):
         jz = (to - zh + 4) % 4
@@ -301,6 +308,7 @@
         total = yown[h]
         for j in range(1, 8):
             remote(ysend.at[0, 0], yrecv.at[h, j], yss.at[0, 0], yrs.at[h, j], core_dev).wait_recv()
+        for j in range(1, 8):
             total = total + unpack(yrecv[h, j])
         for zb in range(2):
             zs[2 * zb + h] = total[4 * zb : 4 * zb + 4]
@@ -371,6 +379,7 @@
             pltpu.VMEM((2, 8, 8, 16, 128), bf),
             pltpu.VMEM((512, 2048), bf),
             pltpu.VMEM((1024, 2048), bf),
+            pltpu.VMEM((2048, 1024), bf),
             pltpu.VMEM((512, COLS), f32),
             pltpu.VMEM((8, 4, 16, PACKED), f32),
             pltpu.VMEM((8, 3, 16, PACKED), f32),

time: 46.8 us -> 45.2 us (0.966)
  Pallas kernels: 45.3 us -> 43.7 us
    pallas_call x1, Pallas kernels: 45.3 us -> 43.7 us  [per_device(): pl.pallas_call(kernel, out_shape=jax.ShapeDtypeStruct((4, 1024), bf), in_...]
where the time goes in v3:
time: 45.2 us; the launch traced here: 45 us
  Pallas kernels  43.7 us (97%)
  local copies, waits for them, and re-layouts  1.3 us (3%)
    pallas_call x1, Pallas kernels, per_device(): pl.pallas_call(kernel, out_shape=jax.ShapeDtypeStruct((4, 1024), bf), in_...  43.7 us
    unnamed x1, local copies, waits for them, and re-layouts  1.3 us

profile of v3, /device:TPU:9, one launch (start us, length us, event | category | flops | bytes accessed | tf_op | source)
XLA Modules:
  0.0 45.0 jit_solution(2393578623103350982)
XLA Ops:
  0.0 43.7 %shard_map.46 = bf16[4,1024]{1,0:T(4,128)(2,1)} custom-call(bf16[128,16,128]{2,1,0:T(8,128)(2,1)} %amps.1, bf16[16,64,16,128]{3,2,1,0:T(8,128)(2,1)} %bitcast.1, s32[8,8]{1,0:T(8,128)} %mask_a_hbm.1, s32[8,8]{1,0:T(8,128)} %mask_i_hbm.1), custom_call_target="tpu_custom_call" | custom-call | flops 2147483648 | bytes 5242880 | tf_op jit(solution)/shard_map/pallas_call | solution.py:369
  43.7 1.3 %copy.6 = bf16[4,1024]{1,0:T(4,128)(2,1)} copy(bf16[4,1024]{1,0:T(4,128)(2,1)} %shard_map.46) | data formatting | bytes 16384

commit v4 on v3

--- a/solution.py
+++ b/solution.py
@@ -138,7 +138,7 @@
             ints_rows(slabs, pl.multiple_of(256 * j + 16 * g, 16))
         return 0
 
-    lax.fori_loop(0, 16, cross, 0, unroll=2)
+    lax.fori_loop(0, 16, cross, 0, unroll=4)
 
     def diagonal(g, _):
         turn = [(r + g + 1) % 16 for r in range(16)]
@@ -150,7 +150,7 @@
         ints_rows(slabs, pl.multiple_of(640 + 16 * g, 16))
         return 0
 
-    lax.fori_loop(0, 8, diagonal, 0, unroll=2)
+    lax.fori_loop(0, 8, diagonal, 0, unroll=4)
     for cp in icopies:
         cp.wait_recv()
 
@@ -167,7 +167,7 @@
         amps_rows(0, 1, n // 4, n % 4, pl.multiple_of(16 * n, 16))
         return 0
 
-    lax.fori_loop(0, 16, early_rows, 0, unroll=4)
+    lax.fori_loop(0, 16, early_rows, 0, unroll=8)
 
     def ladder(row0, rows, turned=False):
         a = flat_a[row0 : row0 + rows, :]
@@ -258,7 +258,7 @@
         flat_t[pl.ds(cols, 256), pl.ds(rows, 256)] = flat_i[pl.ds(rows, 256), pl.ds(cols, 256)].T
         return 0
 
-    lax.fori_loop(0, 32, turn_ints, 0, unroll=2)
+    lax.fori_loop(0, 32, turn_ints, 0, unroll=4)
 
     fwds = []
     for k in range(4):

time: 45.2 us -> 45 us (level)
  no operation moved by 1% of the time
where the time goes in v4:
time: 45 us; the launch traced here: 44.9 us
  Pallas kernels  43.6 us (97%)
  local copies, waits for them, and re-layouts  1.3 us (3%)
    pallas_call x1, Pallas kernels, per_device(): pl.pallas_call(kernel, out_shape=jax.ShapeDtypeStruct((4, 1024), bf), in_...  43.6 us
    unnamed x1, local copies, waits for them, and re-layouts  1.3 us

profile of v4, /device:TPU:9, one launch (start us, length us, event | category | flops | bytes accessed | tf_op | source)
XLA Modules:
  0.0 44.9 jit_solution(16828772334918935601)
XLA Ops:
  0.0 43.6 %shard_map.46 = bf16[4,1024]{1,0:T(4,128)(2,1)} custom-call(bf16[128,16,128]{2,1,0:T(8,128)(2,1)} %amps.1, bf16[16,64,16,128]{3,2,1,0:T(8,128)(2,1)} %bitcast.1, s32[8,8]{1,0:T(8,128)} %mask_a_hbm.1, s32[8,8]{1,0:T(8,128)} %mask_i_hbm.1), custom_call_target="tpu_custom_call" | custom-call | flops 2147483648 | bytes 5242880 | tf_op jit(solution)/shard_map/pallas_call | solution.py:369
  43.6 1.3 %copy.6 = bf16[4,1024]{1,0:T(4,128)(2,1)} copy(bf16[4,1024]{1,0:T(4,128)(2,1)} %shard_map.46) | data formatting | bytes 16384
